TPU v7x, 32 devices: a whole 2x2x4 slice. The times are simulated.
32 devices in a mesh: rows: 16 (over z, y, x), tm: 2 (over core).
Axes of the slice: x: 2, y: 2, z: 4, core: 2. Of those that a mesh axis runs over, the one named last changes fastest.
Arguments:
- snapshots: bfloat16 [262144, 256], P('rows', 'tm'), may hold values from -6 to 6
- basis: bfloat16 [262144, 32], P(('rows', 'tm')), may hold values from -0.01171875 to 0.01171875
Outputs:
- gram: float32 [560, 560], replicated
- rhs: float32 [560, 32], replicated
All inputs are finite; a program needn't handle non-finite values.
Results may differ from a plain program's by a relative error of at most 0.0003.
Values may be sent and summed in bfloat16 or wider, within the bound.
A program may use at most 64 MiB of HBM per device.

v0:
```python
import jax
import jax.numpy as jnp
import numpy as np
from jax import lax
from jax.sharding import PartitionSpec as P


def from_behind(block, axis, distance):
    devices = range(lax.axis_size(axis))
    route = [(i - distance, i) for i in devices if i - distance in devices]
    return lax.ppermute(block, axis, route)


def build_sums(projected, velocity, first_step, total_steps):
    series = projected.T
    num_modes = series.shape[1]
    weight = (first_step + jnp.arange(series.shape[0]) < total_steps - 1).astype(jnp.float32)
    upper_pair = np.triu_indices(num_modes)
    quadratic = series[:, upper_pair[0]] * series[:, upper_pair[1]]
    features = jnp.concatenate([series, quadratic], axis=1)
    weighted = features * weight[:, None]
    gram_part = jnp.dot(weighted.T, features, precision=lax.Precision.HIGHEST)
    rhs_part = jnp.dot(weighted.T, velocity.T, precision=lax.Precision.HIGHEST)
    return (gram_part, rhs_part)


def shards(snapshots, basis):
    rows_count, step_count = snapshots.shape
    partial_value = jnp.einsum(
        "nr,nt->rt",
        lax.all_gather(basis, "tm", axis=0, tiled=True),
        snapshots,
        preferred_element_type=jnp.float32,
    )
    first_next = from_behind(partial_value[:, :1], "tm", -1)
    velocity_part = jnp.concatenate([partial_value[:, 1:], first_next], axis=1) - partial_value
    group_size = lax.axis_size("rows")
    share = step_count // group_size
    total_steps = step_count * lax.axis_size("tm")
    first_step = lax.axis_index("tm") * step_count + lax.axis_index("rows") * share
    whole_proj, whole_vel = lax.psum((partial_value, velocity_part), "rows")
    column = lax.axis_index("rows") * share
    projected = lax.dynamic_slice_in_dim(whole_proj, column, share, 1)
    velocity = lax.dynamic_slice_in_dim(whole_vel, column, share, 1)
    gram_part, rhs_part = build_sums(projected, velocity, first_step, total_steps)
    gram_sum, rhs_sum = lax.psum((gram_part, rhs_part), ("rows", "tm"))
    return (gram_sum / total_steps, rhs_sum / total_steps)


def solution(mesh):
    in_specs = (P("rows", "tm"), P(("rows", "tm"), None))
    out_specs = (P(), P())
    return jax.shard_map(shards, mesh=mesh, in_specs=in_specs, out_specs=out_specs, check_vma=False)
```

profile of v0, /device:TPU:0, one launch (start us, length us, event | category | flops | bytes accessed | tf_op | source)
XLA Modules:
  0.0 249.2 jit_solution(8498607268534217137)
XLA Ops:
  7.2 0.0 all-gather.2.cloned.1.call-start
  7.2 0.7 all-gather.2.cloned.1.call-update
  7.9 0.0 all-reduce.4.cloned.1.call-start
  8.0 0.7 pad_clamp_fusion.1
  8.7 0.7 pad_clamp_fusion
  9.4 12.0 %all-gather.2.cloned.1.call-done = bf16[16384,32]{0,1:T(8,128)(2,1)} async-done(((bf16[8192,32]{0,1:T(8,128)(2,1)}), bf16[16384,32]{0,1:T(8,128)(2,1)}) %all-gather.2.cloned.1.call-update) | async-done | bytes 1048592 | tf_op jit(solution)/shard_map/all_gather | solution.py:31
  21.3 3.3 %fusion.10 = f32[32,128]{1,0:T(8,128)S(1)} fusion(bf16[16384,32]{0,1:T(8,128)(2,1)} %all-gather.2.cloned.1.call-done, bf16[16384,128]{1,0:T(8,128)(2,1)} %param.6), kind=kOutput, calls=%fused_computation.21 | convolution fusion | flops 134217728 | bytes 5259264 | tf_op jit(solution)/shard_map/nr,nt->rt/dot_general | solution.py:29
  24.6 1.3 collective-permute-start
  25.9 0.1 slice.12
  25.9 1.7 collective-permute-done
  27.7 0.1 maximum_subtract_fusion
  27.7 77.0 %all-reduce.1 = (f32[32,128]{1,0:T(8,128)S(1)}, f32[32,128]{1,0:T(8,128)S(1)}) all-reduce(f32[32,128]{1,0:T(8,128)S(1)} %fusion.10, f32[32,128]{1,0:T(8,128)S(1)} %maximum_subtract_fusion), channel_id=1, replica_groups=mesh['rows'=16,'tm'=2] {'rows'}, use_global_device_ids=true, to_apply=%region_0.0 | all-reduce | flops 8192 | bytes 65536 | tf_op jit(solution)/shard_map/psum | solution.py:41
  104.7 0.1 dynamic-slice_bitcast_fusion
  104.8 0.1 copy.8
  104.9 1.6 gather_fusion.1
  106.5 1.6 gather_fusion
  108.1 0.1 copy.9
  108.2 2.6 %fusion.2 = f32[560,560]{1,0:T(8,128)} fusion(f32[8,528]{1,0:T(8,128)S(1)} %copy.9, f32[8,32]{1,0:T(8,128)S(1)} %copy.8, f32[8]{0:T(128)S(1)} %compare_convert_fusion), kind=kOutput, calls=%fused_computation.7 | convolution fusion | flops 30119040 | bytes 1272352 | tf_op jit(solution)/shard_map/dot_general | solution.py:22
  110.8 0.9 fusion
  111.7 0.0 all-reduce.4.cloned.1.call-update
  111.7 127.4 %all-reduce.4.cloned.1.call-done = (f32[560,560]{1,0:T(8,128)}, f32[560,32]{0,1:T(8,128)}) async-done(((f32[560,560]{1,0:T(8,128)}, f32[560,32]{0,1:T(8,128)}), (f32[560,560]{1,0:T(8,128)}, f32[560,32]{0,1:T(8,128)})) %all-reduce.4.cloned.1.call-update) | async-done | bytes 1326096 | tf_op jit(solution)/shard_map/psum | solution.py:46
  239.1 0.0 copy-start
  239.1 2.6 %broadcast_multiply_fusion = f32[560,560]{1,0:T(8,128)} fusion(f32[560,560]{1,0:T(8,128)} %get-tuple-element.2), kind=kLoop, calls=%fused_computation.2 | loop fusion | flops 313600 | bytes 2508800 | tf_op jit(solution)/shard_map/div | solution.py:47
  241.7 0.0 copy-done
  241.7 0.6 broadcast_multiply_fusion.1
  (2 shorter events, 0.0 us)
Async XLA Ops:
  7.2 14.1 %all-gather.2.cloned.1.call-start = ((), (), s32[]{:S(2)}) async-start(), calls=%async_computation | async-start | bytes 1572864 | tf_op jit(solution)/shard_map/all_gather | solution.py:31
  7.9 231.2 %all-reduce.4.cloned.1.call-start = ((), (), s32[]{:S(2)}) async-start(), calls=%async_computation.1 | async-start | bytes 3031040 | tf_op jit(solution)/shard_map/psum | solution.py:46
  24.6 3.1 %collective-permute-start = (f32[32,1]{1,0:T(8,128)S(1)}, f32[32,1]{1,0:T(8,128)S(1)}, u32[]{:S(2)}, u32[]{:S(2)}) collective-permute-start(f32[32,1]{1,0:T(8,128)S(1)} %bitcast.7), channel_id=1, source_target_pairs={{1,0},{3,2},{5,4},{7,6},{9,8},{11,10},{13,12},{15,14},{17,16},{19,... | collective-permute-start | bytes 392 | tf_op jit(solution)/shard_map/ppermute | solution.py:11
  239.1 2.6 %copy-start = (f32[560,32]{0,1:T(8,128)S(1)}, f32[560,32]{0,1:T(8,128)}, u32[]{:S(2)}) copy-start(f32[560,32]{0,1:T(8,128)} %get-tuple-element.3) | copy-start | bytes 215044
Sparse Core Ops, SparseCore 0:
  9.5 11.7 all-gather.1
  111.8 127.2 all-reduce.3
where the time goes:
time: 249 us
  waiting for transfers between devices  142 us (57%)
  blocking collectives  77 us (31%)
  between operations  14.1 us (6%)
  matrix products  6.72 us (3%)
  other arithmetic  4.73 us (2%)
  local copies, waits for them, and re-layouts  3.5 us (1%)
    psum x1, waiting for transfers between devices, shards(): gram_sum, rhs_sum = lax.psum((gram_part, rhs_part), ('rows', 'tm'))  127 us
    psum x1, blocking collectives, shards(): whole_proj, whole_vel = lax.psum((partial_value, velocity_part), 'rows')  77 us
    all_gather x1, waiting for transfers between devices, shards(): lax.all_gather(basis, 'tm', axis=0, tiled=True)  12 us
  transfers between devices with their start and end apart: 3, of which 3 were waited for; matrix products, arithmetic and copies ran while one was open for 1% of the time, Pallas kernels for 0%

commit v1 on v0

--- a/solution.py
+++ b/solution.py
@@ -1,8 +1,18 @@
+import functools
 import jax
 import jax.numpy as jnp
 import numpy as np
 from jax import lax
 from jax.sharding import PartitionSpec as P
+
+
+def _change_area(xs, bus_axis, which_axis):
+    for idx in (bus_axis, which_axis):
+        xs = jax.lax.psum(xs, idx)
+    return xs
+
+
+draw_vectors = functools.partial(_change_area, bus_axis="tm", which_axis="rows")
 
 
 def from_behind(block, axis, distance):
@@ -43,7 +53,7 @@
     projected = lax.dynamic_slice_in_dim(whole_proj, column, share, 1)
     velocity = lax.dynamic_slice_in_dim(whole_vel, column, share, 1)
     gram_part, rhs_part = build_sums(projected, velocity, first_step, total_steps)
-    gram_sum, rhs_sum = lax.psum((gram_part, rhs_part), ("rows", "tm"))
+    gram_sum, rhs_sum = draw_vectors((gram_part, rhs_part))
     return (gram_sum / total_steps, rhs_sum / total_steps)
 
 

time: 249 us -> 262 us (1.052)
  waiting for transfers between devices: 142 us -> 155 us
    psum x1 -> x2, waiting for transfers between devices: 127 us -> 141 us  [_change_area(): xs = jax.lax.psum(xs, idx)]
  transfers between devices with their start and end apart: 3 -> 4, of which waited for: 3 -> 4; matrix products, arithmetic and copies ran while one was open for 1% -> 1% of each run, Pallas kernels for 0% -> 0%
where the time goes in v1:
time: 262 us
  waiting for transfers between devices  155 us (59%)
  blocking collectives  77 us (29%)
  between operations  13.8 us (5%)
  matrix products  6.72 us (3%)
  other arithmetic  4.73 us (2%)
  local copies, waits for them, and re-layouts  3.5 us (1%)
    psum x2, waiting for transfers between devices, _change_area(): xs = jax.lax.psum(xs, idx)  141 us
    psum x1, blocking collectives, shards(): whole_proj, whole_vel = lax.psum((partial_value, velocity_part), 'rows')  77 us
    all_gather x1, waiting for transfers between devices, shards(): lax.all_gather(basis, 'tm', axis=0, tiled=True)  12 us
  transfers between devices with their start and end apart: 4, of which 4 were waited for; matrix products, arithmetic and copies ran while one was open for 1% of the time, Pallas kernels for 0%

profile of v1, /device:TPU:0, one launch (start us, length us, event | category | flops | bytes accessed | tf_op | source)
XLA Modules:
  0.0 262.2 jit_solution(1552404764944095701)
XLA Ops:
  7.2 0.0 all-gather.2.cloned.1.call-start
  7.2 0.7 all-gather.2.cloned.1.call-update
  7.9 0.0 all-reduce.8.cloned.1.call-start
  8.0 0.7 pad_clamp_fusion.1
  8.7 0.7 pad_clamp_fusion
  9.4 12.0 %all-gather.2.cloned.1.call-done = bf16[16384,32]{0,1:T(8,128)(2,1)} async-done(((bf16[8192,32]{0,1:T(8,128)(2,1)}), bf16[16384,32]{0,1:T(8,128)(2,1)}) %all-gather.2.cloned.1.call-update) | async-done | bytes 1048592 | tf_op jit(solution)/shard_map/all_gather | solution.py:41
  21.3 3.3 %fusion.10 = f32[32,128]{1,0:T(8,128)S(1)} fusion(bf16[16384,32]{0,1:T(8,128)(2,1)} %all-gather.2.cloned.1.call-done, bf16[16384,128]{1,0:T(8,128)(2,1)} %param.6), kind=kOutput, calls=%fused_computation.21 | convolution fusion | flops 134217728 | bytes 5259264 | tf_op jit(solution)/shard_map/nr,nt->rt/dot_general | solution.py:39
  24.6 1.3 collective-permute-start
  25.9 0.1 slice.12
  25.9 1.7 collective-permute-done
  27.7 0.1 maximum_subtract_fusion
  27.7 77.0 %all-reduce = (f32[32,128]{1,0:T(8,128)S(1)}, f32[32,128]{1,0:T(8,128)S(1)}) all-reduce(f32[32,128]{1,0:T(8,128)S(1)} %fusion.10, f32[32,128]{1,0:T(8,128)S(1)} %maximum_subtract_fusion), channel_id=1, replica_groups=mesh['rows'=16,'tm'=2] {'rows'}, use_global_device_ids=true, to_apply=%region_0.0 | all-reduce | flops 8192 | bytes 65536 | tf_op jit(solution)/shard_map/psum | solution.py:51
  104.7 0.1 dynamic-slice_bitcast_fusion
  104.8 0.1 copy.8
  104.9 1.6 gather_fusion.1
  106.5 1.6 gather_fusion
  108.1 0.1 copy.9
  108.2 2.6 fusion.2
  110.8 0.9 fusion
  111.7 0.0 all-reduce.8.cloned.1.call-update
  111.7 0.0 all-reduce.6.cloned.1.call-start
  111.7 16.4 %all-reduce.8.cloned.1.call-done = (f32[560,560]{1,0:T(8,128)}, f32[560,32]{0,1:T(8,128)}) async-done(((f32[560,560]{1,0:T(8,128)}, f32[560,32]{0,1:T(8,128)}), (f32[560,560]{1,0:T(8,128)}, f32[560,32]{0,1:T(8,128)})) %all-reduce.8.cloned.1.call-update) | async-done | bytes 1326096 | tf_op jit(solution)/shard_map/psum | solution.py:11
  128.1 0.0 all-reduce.6.cloned.1.call-update
  128.1 124.3 %all-reduce.6.cloned.1.call-done = (f32[560,560]{1,0:T(8,128)}, f32[560,32]{0,1:T(8,128)}) async-done(((f32[560,560]{1,0:T(8,128)}, f32[560,32]{0,1:T(8,128)}), (f32[560,560]{1,0:T(8,128)}, f32[560,32]{0,1:T(8,128)})) %all-reduce.6.cloned.1.call-update) | async-done | bytes 1326096 | tf_op jit(solution)/shard_map/psum | solution.py:11
  252.4 0.0 copy-start
  252.4 2.6 broadcast_multiply_fusion
  255.0 0.0 copy-done
  255.0 0.6 broadcast_multiply_fusion.1
  (2 shorter events, 0.0 us)
Async XLA Ops:
  7.2 14.1 %all-gather.2.cloned.1.call-start = ((), (), s32[]{:S(2)}) async-start(), calls=%async_computation | async-start | bytes 1572864 | tf_op jit(solution)/shard_map/all_gather | solution.py:41
  7.9 120.2 %all-reduce.8.cloned.1.call-start = ((), (), s32[]{:S(2)}) async-start(), calls=%async_computation.2 | async-start | bytes 3031040 | tf_op jit(solution)/shard_map/psum | solution.py:11
  24.6 3.1 %collective-permute-start = (f32[32,1]{1,0:T(8,128)S(1)}, f32[32,1]{1,0:T(8,128)S(1)}, u32[]{:S(2)}, u32[]{:S(2)}) collective-permute-start(f32[32,1]{1,0:T(8,128)S(1)} %bitcast.7), channel_id=1, source_target_pairs={{1,0},{3,2},{5,4},{7,6},{9,8},{11,10},{13,12},{15,14},{17,16},{19,... | collective-permute-start | bytes 392 | tf_op jit(solution)/shard_map/ppermute | solution.py:21
  111.7 140.7 %all-reduce.6.cloned.1.call-start = ((), (), s32[]{:S(2)}) async-start(), calls=%async_computation.1 | async-start | bytes 3031040 | tf_op jit(solution)/shard_map/psum | solution.py:11
  252.4 2.6 copy-start
Sparse Core Ops, SparseCore 0:
  9.5 11.7 all-gather.1
  111.8 16.2 all-reduce.7
  133.7 118.6 all-reduce.5
